TPU v7x, 32 devices: a whole 2x2x4 slice. The times are simulated.
32 devices in a mesh: row: 4 (over y, x), col: 8 (over z, core).
Axes of the slice: x: 2, y: 2, z: 4, core: 2. Of those that a mesh axis runs over, the one named last changes fastest.
Arguments:
- matrix_band: bfloat16 [48, 16, 128, 128], P('col', 'row'), may hold values from -9 to 9, as said below
- pattern: int32 [48, 16], P('col', 'row'), may hold values 0 or 1
- filter_mask: int32 [48, 16], P('col', 'row'), may hold values 0 or 1
Outputs:
- sign_iterate: bfloat16 [48, 16, 128, 128], P('col', 'row')
Inputs may be any that keep to these rules, and one draw needn't show every extreme that they name: `matrix_band`: the tile at offset 0 of every block row is symmetric.
All inputs are finite; a program needn't handle non-finite values. No bound on the sum of `pattern` or of `filter_mask` on one device may be relied on, other than what follows from the above.
Results may differ from a plain program's by a relative error of at most 0.0031.
Values may be sent and summed in bfloat16 or wider, within the bound.
A program may use at most 192 MiB of HBM per device.

v0:
```python
import math

import jax
import jax.numpy as jnp
from jax import lax
from jax.sharding import PartitionSpec as P


def shifted(value, axis, steps):
    count = lax.axis_size(axis)
    pairs = [(source, (source + steps) % count) for source in range(count)]
    return lax.ppermute(value, axis, pairs)


def whole_rows(window, reach_rows, row_count, band_width):
    mirrored = [
        jnp.swapaxes(window[reach_rows - offset : reach_rows - offset + row_count, offset], -1, -2)
        for offset in range(band_width - 1, 0, -1)
    ]
    upper_part = window[reach_rows : reach_rows + row_count]
    return jnp.concatenate([jnp.stack(mirrored, axis=1), upper_part], axis=1)


def band_product(left_rows, right_rows, start_offset, local_width, band_width):
    row_count = left_rows.shape[0]
    tile_size = left_rows.shape[2]
    zero_tiles = jnp.zeros((row_count, band_width - 1, tile_size, tile_size), left_rows.dtype)
    left_padded = jnp.concatenate([left_rows, zero_tiles], axis=1)
    results = []
    for offset_step in range(local_width):
        offset = start_offset + offset_step
        left_block = lax.dynamic_slice_in_dim(left_padded, offset, 2 * band_width - 1, 1)
        right_block = lax.dynamic_slice_in_dim(right_rows, offset, row_count, 0)
        results.append(
            jnp.einsum(
                "iapq,iarq->ipr", left_block, right_block, preferred_element_type=jnp.float32
            )
        )
    return jnp.stack(results, axis=1)


def on_device(matrix_band, pattern, filter_mask):
    row_count = matrix_band.shape[0]
    local_width = matrix_band.shape[1]
    tile_size = matrix_band.shape[2]
    band_width = local_width * lax.axis_size("row")
    reach_rows = band_width - 1
    hop_count = (reach_rows + row_count - 1) // row_count
    factor = 1.0 / math.sqrt((2 * band_width - 1) * tile_size)
    hop_spans = [
        (distance, min(row_count, reach_rows - (distance - 1) * row_count))
        for distance in range(1, hop_count + 1)
    ]
    masked = matrix_band * pattern[:, :, None, None].astype(jnp.bfloat16)
    own_rows = lax.all_gather(masked, "row", axis=1, tiled=True)
    behind_parts = [
        shifted(own_rows[row_count - piece_rows :], "col", distance)
        for distance, piece_rows in hop_spans
    ]
    ahead_parts = [
        shifted(own_rows[:piece_rows], "col", -distance) for distance, piece_rows in hop_spans
    ]
    window = jnp.concatenate(behind_parts[::-1] + [own_rows] + ahead_parts, axis=0)
    matrix_rows_all = whole_rows(window, reach_rows, row_count + reach_rows, band_width)
    left_rows = matrix_rows_all[:row_count]
    start_offset = lax.axis_index("row") * local_width
    square_sum = band_product(left_rows, matrix_rows_all, start_offset, local_width, band_width)
    square = (
        filter_mask[:, :, None, None].astype(jnp.float32) * (factor * factor) * square_sum
    ).astype(jnp.bfloat16)
    square_own = lax.all_gather(square, "row", axis=1, tiled=True)
    square_parts = [
        shifted(square_own[row_count - piece_rows :], "col", distance)
        for distance, piece_rows in hop_spans
    ]
    square_window = jnp.concatenate(square_parts[::-1] + [square_own], axis=0)
    square_rows_all = whole_rows(square_window, reach_rows, row_count, band_width)
    cube = band_product(square_rows_all, matrix_rows_all, start_offset, local_width, band_width)
    result = (
        pattern[:, :, None, None].astype(jnp.float32)
        * 0.5
        * (3.0 * masked.astype(jnp.float32) - cube)
    )
    return result.astype(jnp.bfloat16)


def solution(mesh):
    placed = (P("col", "row", None, None), P("col", "row"), P("col", "row"))
    return jax.shard_map(
        on_device,
        mesh=mesh,
        in_specs=placed,
        out_specs=P("col", "row", None, None),
        check_vma=False,
    )
```

profile of v0, /device:TPU:0, one launch (start us, length us, event | category | flops | bytes accessed | tf_op | source)
XLA Modules:
  0.0 743.5 jit_solution(10605452930024016221)
XLA Ops:
  7.3 2.1 broadcast_multiply_fusion
  9.5 46.8 %all-gather.3.cloned.1.call-done = bf16[6,16,128,128]{3,2,1,0:T(8,128)(2,1)} async-done(((bf16[6,4,128,128]{3,2,1,0:T(8,128)(2,1)}), bf16[6,16,128,128]{3,2,1,0:T(8,128)(2,1)}) %all-gather.3.cloned.1.call-update) | async-done | bytes 3145744 | tf_op jit(solution)/shard_map/all_gather | solution.py:55
  56.3 1.5 collective-permute-start.1
  57.8 3.5 collective-permute-start.3
  61.4 4.0 fusion.84
  65.4 1.5 collective-permute-start.4
  67.6 160.8 %collective-permute-done = bf16[3,16,128,128]{3,2,1,0:T(8,128)(2,1)} collective-permute-done((bf16[3,16,128,128]{3,2,1,0:T(8,128)(2,1)}, bf16[3,16,128,128]{3,2,1,0:T(8,128)(2,1)}, u32[]{:S(2)}, u32[]{:S(2)}) %collective-permute-start) | collective-permute-done | bytes 1572896 | tf_op jit(solution)/shard_map/ppermute | solution.py:12
  228.4 1.5 constant_dynamic-update-slice_fusion.4
  229.9 7.2 constant_dynamic-update-slice_fusion.13
  237.1 4.9 copy-done.11
  243.0 8.5 %constant_dynamic-update-slice_fusion.22 = (bf16[27,16,128,128]{3,2,1,0:T(8,128)(2,1)}, bf16[24,16,128,128]{3,2,1,0:T(8,128)(2,1)S(1)}, bf16[30,16,128,128]{3,2,...) fusion(bf16[6,16,128,128]{3,2,1,0:T(8,128)(2,1)} %copy-done.1, ...), kind=kLoop, calls=%fused_computation.112 | loop fusion | bytes 18874368
  251.5 6.6 constant_dynamic-update-slice_fusion.21
  258.1 8.4 %constant_dynamic-update-slice_fusion.20 = (bf16[27,16,128,128]{3,2,1,0:T(8,128)(2,1)}, bf16[24,16,128,128]{3,2,1,0:T(8,128)(2,1)S(1)}, bf16[30,16,128,128]{3,2,...) fusion(bf16[27,16,128,128]{3,2,1,0:T(8,128)(2,1)} %get-tuple-element.31, ...), kind=kLoop, calls=%fused_computation.110 | loop fusion | bytes 18874368
  266.5 30.3 %collective-permute-done.4 = bf16[6,16,128,128]{3,2,1,0:T(8,128)(2,1)} collective-permute-done((bf16[6,16,128,128]{3,2,1,0:T(8,128)(2,1)}, bf16[6,16,128,128]{3,2,1,0:T(8,128)(2,1)}, u32[]{:S(2)}, u32[]{:S(2)}) %collective-permute-start.4) | collective-permute-done | bytes 3145760 | tf_op jit(solution)/shard_map/ppermute | solution.py:12
  296.8 7.2 constant_dynamic-update-slice_fusion.19
  304.0 3.3 slice_bitcast_fusion.2
  307.3 2.2 copy.38
  309.6 4.2 slice_bitcast_fusion.8
  313.8 2.2 copy.32
  316.0 2.0 fusion.55
  318.0 2.2 copy.31
  320.3 2.2 copy.33
  322.5 2.2 copy.34
  324.7 2.2 copy.35
  326.9 2.2 copy.36
  329.2 2.2 copy.37
  331.4 2.2 copy.39
  333.6 2.2 copy.40
  335.8 2.2 copy.41
  338.1 2.2 copy.42
  340.3 2.2 copy.43
  342.5 2.2 constant_dynamic-update-slice_fusion.37
  344.7 19.5 %collective-permute-done.5 = bf16[3,16,128,128]{3,2,1,0:T(8,128)(2,1)} collective-permute-done((bf16[3,16,128,128]{3,2,1,0:T(8,128)(2,1)}, bf16[3,16,128,128]{3,2,1,0:T(8,128)(2,1)}, u32[]{:S(2)}, u32[]{:S(2)}) %collective-permute-start.5) | collective-permute-done | bytes 1572896 | tf_op jit(solution)/shard_map/ppermute | solution.py:12
  364.2 2.7 constant_dynamic-update-slice_fusion.18
  366.9 2.5 slice_bitcast_fusion
  369.5 2.2 copy.44
  371.7 2.2 copy.45
  374.0 2.3 constant_dynamic-update-slice_fusion.36
  376.2 2.1 constant_dynamic-update-slice_fusion.35
  378.4 2.1 constant_dynamic-update-slice_fusion.34
  380.5 2.1 constant_dynamic-update-slice_fusion.33
  382.6 2.1 constant_dynamic-update-slice_fusion.32
  384.8 2.1 constant_dynamic-update-slice_fusion.31
  386.9 2.1 constant_dynamic-update-slice_fusion.30
  396.3 10.3 %maximum_dynamic-update-slice_fusion = bf16[21,31,128,128]{3,2,1,0:T(8,128)(2,1)} fusion(bf16[21,31,128,128]{3,2,1,0:T(8,128)(2,1)} %constant_dynamic-update-slice_fusion.23, bf16[3,16,128,128]{3,2,1,0:T(8,128)(2,1)} %collective-permute-done.5, bf16[6,16,128,128]{3,2,1,0:T(8,128)(2,1)} %collective-permute-done.4, ...), kind=kLoop, calls=%fused_computation | loop fusion | flops 44040192 | bytes 22020096 | tf_op jit(solution)/shard_map/concatenate | solution.py:21
  406.6 4.0 slice.182
  410.6 4.5 fusion.52
  415.2 4.5 fusion.49
  419.7 4.5 fusion.46
  424.3 4.5 fusion.43
  429.9 111.7 %all-gather.5.cloned.1.call-done = bf16[6,16,128,128]{3,2,0,1:T(8,128)(2,1)} async-done(((bf16[6,4,128,128]{3,2,0,1:T(8,128)(2,1)}), bf16[6,16,128,128]{3,2,0,1:T(8,128)(2,1)}) %all-gather.5.cloned.1.call-update) | async-done | bytes 3145744 | tf_op jit(solution)/shard_map/all_gather | solution.py:71
  541.6 3.5 copy.46
  545.1 1.5 collective-permute-start.7
  546.7 1.3 slice.183
  547.9 2.7 collective-permute-start.6
  550.7 150.4 %collective-permute-done.6 = bf16[3,16,128,128]{2,3,0,1:T(8,128)(2,1)} collective-permute-done((bf16[3,16,128,128]{2,3,0,1:T(8,128)(2,1)}, bf16[3,16,128,128]{2,3,0,1:T(8,128)(2,1)}, u32[]{:S(2)}, u32[]{:S(2)}) %collective-permute-start.6) | collective-permute-done | bytes 1572896 | tf_op jit(solution)/shard_map/ppermute | solution.py:12
  701.2 1.5 constant_dynamic-update-slice_fusion.39
  702.7 3.6 constant_dynamic-update-slice_fusion.41
  707.4 2.5 constant_dynamic-update-slice_fusion.40
  717.0 4.6 fusion.23
  721.6 4.6 fusion.28
  726.2 4.6 fusion.33
  730.7 4.6 fusion.38
  735.4 1.3 fusion.22
  (68 shorter events, 19.2 us)
Async XLA Ops:
  6.5 49.8 %all-gather.3.cloned.1.call-start = ((), (), s32[]{:S(2)}) async-start(), calls=%async_computation | async-start | bytes 3932160 | tf_op jit(solution)/shard_map/all_gather | solution.py:55
  9.5 532.1 %all-gather.5.cloned.1.call-start = ((), (), s32[]{:S(2)}) async-start(), calls=%async_computation.1 | async-start | bytes 3932160 | tf_op jit(solution)/shard_map/all_gather | solution.py:71
  56.3 173.6 %collective-permute-start.1 = (bf16[6,16,128,128]{3,2,1,0:T(8,128)(2,1)}, bf16[6,16,128,128]{3,2,1,0:T(8,128)(2,1)}, u32[]{:S(2)}, u32[]{:S(2)}) collective-permute-start(bf16[6,16,128,128]{3,2,1,0:T(8,128)(2,1)} %all-gather.3.cloned.1.call-done), channel_id=1, source_target_pairs={{0,2},{1,3},{2,4},{3,5},{4,6},{5,7},{6,0},{7,1},{8,10},{9,11},{10,... | collective-permute-start | bytes 9437192 | tf_op jit(solution)/shard_map/ppermute | solution.py:12
  57.8 179.3 %collective-permute-start.2 = (bf16[6,16,128,128]{3,2,1,0:T(8,128)(2,1)}, bf16[6,16,128,128]{3,2,1,0:T(8,128)(2,1)S(1)}, u32[]{:S(2)}, u32[]{:S(2)}) collective-permute-start(bf16[6,16,128,128]{3,2,1,0:T(8,128)(2,1)} %all-gather.3.cloned.1.call-done), channel_id=1, source_target_pairs={{0,1},{1,2},{2,3},{3,4},{4,5},{5,6},{6,7},{7,0},{8,9},{9,10},{10,1... | collective-permute-start | bytes 9437192 | tf_op jit(solution)/shard_map/ppermute | solution.py:12
  57.8 200.3 %collective-permute-start.3 = (bf16[6,16,128,128]{3,2,1,0:T(8,128)(2,1)}, bf16[6,16,128,128]{3,2,1,0:T(8,128)(2,1)}, u32[]{:S(2)}, u32[]{:S(2)}) collective-permute-start(bf16[6,16,128,128]{3,2,1,0:T(8,128)(2,1)} %all-gather.3.cloned.1.call-done), channel_id=1, source_target_pairs={{0,7},{1,0},{2,1},{3,2},{4,3},{5,4},{6,5},{7,6},{8,15},{9,8},{10,9... | collective-permute-start | bytes 9437192 | tf_op jit(solution)/shard_map/ppermute | solution.py:12
  65.4 163.0 %collective-permute-start = (bf16[3,16,128,128]{3,2,1,0:T(8,128)(2,1)}, bf16[3,16,128,128]{3,2,1,0:T(8,128)(2,1)}, u32[]{:S(2)}, u32[]{:S(2)}) collective-permute-start(bf16[3,16,128,128]{3,2,1,0:T(8,128)(2,1)} %get-tuple-element.22), channel_id=1, source_target_pairs={{0,3},{1,4},{2,5},{3,6},{4,7},{5,0},{6,1},{7,2},{8,11},{9,12},{10,... | collective-permute-start | bytes 4718600 | tf_op jit(solution)/shard_map/ppermute | solution.py:12
  65.4 231.4 %collective-permute-start.4 = (bf16[6,16,128,128]{3,2,1,0:T(8,128)(2,1)}, bf16[6,16,128,128]{3,2,1,0:T(8,128)(2,1)}, u32[]{:S(2)}, u32[]{:S(2)}) collective-permute-start(bf16[6,16,128,128]{3,2,1,0:T(8,128)(2,1)} %all-gather.3.cloned.1.call-done), channel_id=1, source_target_pairs={{0,6},{1,7},{2,0},{3,1},{4,2},{5,3},{6,4},{7,5},{8,14},{9,15},{10,... | collective-permute-start | bytes 9437192 | tf_op jit(solution)/shard_map/ppermute | solution.py:12
  228.4 135.8 %collective-permute-start.5 = (bf16[3,16,128,128]{3,2,1,0:T(8,128)(2,1)}, bf16[3,16,128,128]{3,2,1,0:T(8,128)(2,1)}, u32[]{:S(2)}, u32[]{:S(2)}) collective-permute-start(bf16[3,16,128,128]{3,2,1,0:T(8,128)(2,1)} %get-tuple-element.21), channel_id=1, source_target_pairs={{0,5},{1,6},{2,7},{3,0},{4,1},{5,2},{6,3},{7,4},{8,13},{9,14},{10,... | collective-permute-start | bytes 4718600 | tf_op jit(solution)/shard_map/ppermute | solution.py:12
  237.1 4.9 copy-start.11
  237.1 5.9 copy-start.1
  243.0 8.5 %copy-start = (bf16[6,16,128,128]{3,2,1,0:T(8,128)(2,1)S(1)}, bf16[6,16,128,128]{3,2,1,0:T(8,128)(2,1)}, u32[]{:S(2)}) copy-start(bf16[6,16,128,128]{3,2,1,0:T(8,128)(2,1)} %all-gather.3.cloned.1.call-done) | copy-start | bytes 9437188
  373.9 15.1 %copy-start.8 = (bf16[21,1,128,128]{3,2,1,0:T(8,128)(2,1)S(1)}, bf16[21,1,128,128]{3,2,1,0:T(8,128)(2,1)}, u32[]{:S(2)}) copy-start(bf16[21,1,128,128]{3,2,1,0:T(8,128)(2,1)} %copy.39) | copy-start | bytes 2064388
  373.9 16.1 %copy-start.7 = (bf16[21,1,128,128]{3,2,1,0:T(8,128)(2,1)S(1)}, bf16[21,1,128,128]{3,2,1,0:T(8,128)(2,1)}, u32[]{:S(2)}) copy-start(bf16[21,1,128,128]{3,2,1,0:T(8,128)(2,1)} %copy.40) | copy-start | bytes 2064388
  373.9 17.2 %copy-start.6 = (bf16[21,1,128,128]{3,2,1,0:T(8,128)(2,1)S(1)}, bf16[21,1,128,128]{3,2,1,0:T(8,128)(2,1)}, u32[]{:S(2)}) copy-start(bf16[21,1,128,128]{3,2,1,0:T(8,128)(2,1)} %copy.41) | copy-start | bytes 2064388
  373.9 18.2 %copy-start.4 = (bf16[21,1,128,128]{3,2,1,0:T(8,128)(2,1)S(1)}, bf16[21,1,128,128]{3,2,1,0:T(8,128)(2,1)}, u32[]{:S(2)}) copy-start(bf16[21,1,128,128]{3,2,1,0:T(8,128)(2,1)} %copy.42) | copy-start | bytes 2064388
  373.9 19.3 %copy-start.5 = (bf16[21,1,128,128]{3,2,1,0:T(8,128)(2,1)S(1)}, bf16[21,1,128,128]{3,2,1,0:T(8,128)(2,1)}, u32[]{:S(2)}) copy-start(bf16[21,1,128,128]{3,2,1,0:T(8,128)(2,1)} %copy.43) | copy-start | bytes 2064388
  373.9 20.3 %copy-start.9 = (bf16[21,1,128,128]{3,2,1,0:T(8,128)(2,1)S(1)}, bf16[21,1,128,128]{3,2,1,0:T(8,128)(2,1)}, u32[]{:S(2)}) copy-start(bf16[21,1,128,128]{3,2,1,0:T(8,128)(2,1)} %copy.44) | copy-start | bytes 2064388
  374.0 21.3 %copy-start.10 = (bf16[21,1,128,128]{3,2,1,0:T(8,128)(2,1)S(1)}, bf16[21,1,128,128]{3,2,1,0:T(8,128)(2,1)}, u32[]{:S(2)}) copy-start(bf16[21,1,128,128]{3,2,1,0:T(8,128)(2,1)} %copy.45) | copy-start | bytes 2064388
  428.8 121.8 %copy-start.12 = (s32[6,4]{0,1:T(4,128)S(1)}, s32[6,4]{0,1:T(4,128)}, u32[]{:S(2)}) copy-start(s32[6,4]{0,1:T(4,128)} %param.4) | copy-start | bytes 292
  545.1 157.6 %collective-permute-start.7 = (bf16[6,16,128,128]{2,3,0,1:T(8,128)(2,1)S(1)}, bf16[6,16,128,128]{2,3,0,1:T(8,128)(2,1)}, u32[]{:S(2)}, u32[]{:S(2)}) collective-permute-start(bf16[6,16,128,128]{2,3,0,1:T(8,128)(2,1)S(1)} %copy.46), channel_id=1, source_target_pairs={{0,2},{1,3},{2,4},{3,5},{4,6},{5,7},{6,0},{7,1},{8,10},{9,11},{10,... | collective-permute-start | bytes 9437192 | tf_op jit(solution)/shard_map/ppermute | solution.py:12
  546.7 160.7 %collective-permute-start.8 = (bf16[6,16,128,128]{2,3,0,1:T(8,128)(2,1)S(1)}, bf16[6,16,128,128]{2,3,0,1:T(8,128)(2,1)}, u32[]{:S(2)}, u32[]{:S(2)}) collective-permute-start(bf16[6,16,128,128]{2,3,0,1:T(8,128)(2,1)S(1)} %copy.46), channel_id=1, source_target_pairs={{0,1},{1,2},{2,3},{3,4},{4,5},{5,6},{6,7},{7,0},{8,9},{9,10},{10,1... | collective-permute-start | bytes 9437192 | tf_op jit(solution)/shard_map/ppermute | solution.py:12
  547.9 153.2 %collective-permute-start.6 = (bf16[3,16,128,128]{2,3,0,1:T(8,128)(2,1)}, bf16[3,16,128,128]{2,3,0,1:T(8,128)(2,1)}, u32[]{:S(2)}, u32[]{:S(2)}) collective-permute-start(bf16[3,16,128,128]{2,3,0,1:T(8,128)(2,1)} %slice.183), channel_id=1, source_target_pairs={{0,3},{1,4},{2,5},{3,6},{4,7},{5,0},{6,1},{7,2},{8,11},{9,12},{10,... | collective-permute-start | bytes 4718600 | tf_op jit(solution)/shard_map/ppermute | solution.py:12
  712.9 2.7 copy-start.2
  730.7 4.6 copy-start.3
Sparse Core Ops, SparseCore 0:
  9.6 46.6 all-gather.2
  430.0 111.5 all-gather.4
where the time goes:
time: 746 us; the launch traced here: 744 us
  waiting for transfers between devices  520 us (70%)
  local copies, waits for them, and re-layouts  140 us (19%)
  matrix products  36.4 us (5%)
  other arithmetic  22.8 us (3%)
  between operations  13.7 us (2%)
  starting transfers between devices  10.8 us (1%)
    ppermute x9, waiting for transfers between devices, shifted(): return lax.ppermute(value, axis, pairs)  361 us
    all_gather x1, waiting for transfers between devices, on_device(): square_own = lax.all_gather(square, 'row', axis=1, tiled=True)  112 us
    unnamed x60, local copies, waits for them, and re-layouts  77.5 us
    all_gather x1, waiting for transfers between devices, on_device(): own_rows = lax.all_gather(masked, 'row', axis=1, tiled=True)  46.8 us
    another operation x18, local copies, waits for them, and re-layouts, whole_rows(): return jnp.concatenate([jnp.stack(mirrored, axis=1), upper_part], axis=1)  43.5 us
    dot_general x8, matrix products, band_product(): jnp.einsum('iapq,iarq->ipr', left_block, right_block, preferred_element_t...  36.4 us
  transfers between devices with their start and end apart: 11, of which 6 were waited for; matrix products, arithmetic and copies ran while one was open for 12% of the time, Pallas kernels for 0%

commit v1 on v0

v1 whole, which is shorter than its diff:
```python
import functools
import math

import jax
import jax.numpy as jnp
from jax import lax
from jax.experimental import pallas as pl
from jax.experimental.pallas import tpu as pltpu
from jax.sharding import PartitionSpec as P

MESH = pl.DeviceIdType.MESH
SLOTS = 7


def plan(matrix_band):
    rows, width, tile = matrix_band.shape[0], matrix_band.shape[1], matrix_band.shape[2]
    return rows, width, tile, rows // 2


def gather_kernel(R, C, n, lw, T, band_ref, pat_ref, fm_ref, g_ref, x_ref, local_sem, recv, zsend, rsend, ssend, ):
    r = lax.axis_index("row")
    c = lax.axis_index("col")
    core = lax.rem(c, 2)
    half = n // 2
    sib = c + 1 - 2 * core
    right, left = lax.rem(c + 2, C), lax.rem(c + C - 2, C)
    third = lax.rem(c + C - 3 + 6 * core, C)
    others = [lax.rem(r + d, R) for d in range(1, R)]

    barrier = pltpu.get_barrier_semaphore()
    partners = [(r, sib), (r, right), (r, left), (r, third)] + [(o, c) for o in others]
    for p in partners:
        pl.semaphore_signal(barrier, inc=1, device_id=p, device_id_type=MESH)

    for h in range(half):
        for a in range(2):
            i = 2 * h + a
            for t in range(lw):
                m = pat_ref[i, t].astype(jnp.float32)
                tile = band_ref[i, t].astype(jnp.float32) * m
                x_ref[h, a, t * T:(t + 1) * T, :] = tile.astype(jnp.bfloat16)
            pos = lax.broadcasted_iota(jnp.int32, (16, 128), 0)
            mask = jnp.zeros((16, 128), jnp.float32)
            for t in range(lw):
                mask = jnp.where(pos == t, fm_ref[i, t].astype(jnp.float32), mask)
            x_ref[h, a, lw * T:lw * T + 16, :] = mask.astype(jnp.bfloat16)

    pl.semaphore_wait(barrier, len(partners))

    def remote(src, g, rr, send_sem, dev):
        return pltpu.make_async_remote_copy(
            src_ref=src, dst_ref=g_ref.at[g, rr], send_sem=send_sem,
            recv_sem=recv.at[g, rr], device_id=dev, device_id_type=MESH)

    def when(cond, fn):
        if cond is True:
            fn()
        else:
            pl.when(cond)(fn)

    def arrived(g, rr):
        pltpu.make_async_copy(g_ref.at[g, rr], g_ref.at[g, rr], recv.at[g, rr]).wait()

    def g5(h, rr):
        return 2 * h + rr * lw <= 15 - 6 * core

    def g6(h, rr):
        return 2 * h + rr * lw <= 3

    own = lambda h: x_ref.at[h]
    sends = []

    def start(cond, make, waiters):
        when(cond, lambda: make().start())
        sends.append((cond, make))

    for h in range(half):
        start(True, lambda h=h: remote(own(h), half + h, r, zsend.at[0, h], (r, right)), sends)
        start(g5(h, r), lambda h=h: remote(own(h), 5 * half + h, r, zsend.at[1, h], (r, left)), sends)
    for h in range(half):
        if h >= 1:
            start(core == 1, lambda h=h: remote(own(h), h, r, zsend.at[2, h], (r, third)), sends)
        if h <= 1:
            start((core == 0) & g6(h, r),
                  lambda h=h: remote(own(h), 6 * half + h, r, zsend.at[2, h], (r, third)), sends)
    for h in range(half):
        for d, o in enumerate(others):
            start(True, lambda h=h, d=d, o=o: remote(own(h), 3 * half + h, r, rsend.at[3, h, d], (o, c)), sends)
        start(True, lambda h=h: remote(own(h), (4 * core + 2 * (1 - core)) * half + h, r,
                                       ssend.at[1, h, r], (r, sib)), sends)
        pltpu.make_async_copy(own(h), g_ref.at[3 * half + h, r], local_sem.at[h]).start()

    def to_row(cond, q, g, h):
        for d, o in enumerate(others):
            start(cond, lambda d=d, o=o: remote(g_ref.at[g, r], g, r, rsend.at[q, h, d], (o, c)), sends)

    def to_sib(q, s, h, rr):
        g = s * half + h
        dst = (s - 1 + 2 * core) * half + h
        if s == 1:
            cond = True if h >= 1 else core == 1
        elif s == 3:
            cond = True
        else:
            low = (core == 0) & (2 * h + rr * lw <= 15)
            cond = low | ((core == 1) & (2 * h + rr * lw <= 3)) if h <= 1 else low
        start(cond, lambda: remote(g_ref.at[g, rr], dst, rr, ssend.at[q, h, rr], (r, sib)), sends)

    for h in range(half):
        arrived(half + h, r)
        to_row(True, 0, half + h, h)
        to_sib(0, 1, h, r)
        when(g5(h, r), lambda h=h: arrived(5 * half + h, r))
        to_row(g5(h, r), 1, 5 * half + h, h)
        to_sib(2, 5, h, r)
        for o in others:
            arrived(3 * half + h, o)
            to_sib(1, 3, h, o)
    for h in range(half):
        if h >= 1:
            when(core == 0, lambda h=h: arrived(h, r))
            to_row(core == 0, 2, h, h)
        if h <= 1:
            cond = (core == 1) & g6(h, r)
            when(cond, lambda h=h: arrived(6 * half + h, r))
            to_row(cond, 2, 6 * half + h, h)
    for h in range(half):
        for o in others:
            arrived(half + h, o)
            to_sib(0, 1, h, o)
            when(g5(h, o), lambda h=h, o=o: arrived(5 * half + h, o))
            to_sib(2, 5, h, o)
    for h in range(half):
        for o in others:
            if h >= 1:
                when(core == 0, lambda h=h, o=o: arrived(h, o))
            if h <= 1:
                when((core == 1) & g6(h, o), lambda h=h, o=o: arrived(6 * half + h, o))
    for h in range(half):
        for rr in range(R):
            arrived(2 * half + h, rr)
            when((core == 0) | (2 * h + rr * lw <= 15), lambda h=h, rr=rr: arrived(4 * half + h, rr))
            if h <= 1 and 2 * h + rr * lw <= 3:
                when(core == 0, lambda h=h, rr=rr: arrived(6 * half + h, rr))
            if h >= 1:
                when(core == 1, lambda h=h, rr=rr: arrived(h, rr))
    for cond, make in sends:
        when(cond, lambda make=make: make().wait_send())
    for h in range(half):
        pltpu.make_async_copy(own(h), g_ref.at[3 * half + h, r], local_sem.at[h]).wait()


def compute_kernel(R, n, lw, T, W, g_ref, pat_ref, out_ref, a_ref, p_ref, m_ref, acc_ref):
    r = lax.axis_index("row")
    S = 2 * T
    half = n // 2
    M = n * T
    NL = SLOTS * half - 2
    factor = 1.0 / math.sqrt((2 * W - 1) * T)
    scale = factor * factor
    mid = W // 2

    def up(L, e, a):
        return g_ref[L + 1, e // lw, a, (e % lw) * T:(e % lw + 1) * T, :]

    def mask_row(L, e, a):
        return g_ref[L + 1, e // lw, a, lw * T:lw * T + 16, :].astype(jnp.float32)[e % lw:e % lw + 1, :]

    zero = jnp.zeros((T, T), jnp.bfloat16)

    @pl.loop(0, NL + 2)
    def _(L):
        a_ref[L] = jnp.zeros((M, S), jnp.bfloat16)
        m_ref[L] = jnp.zeros((n, 8, S), jnp.float32)

    p_ref[0] = jnp.zeros((M, S), jnp.bfloat16)
    p_ref[NL + 1] = jnp.zeros((M, S), jnp.bfloat16)

    @pl.loop(0, half)
    def _(I):
        for a in range(2):
            i = pl.multiple_of((2 * I + a) * T, T)
            for e in range(W):
                col, b = (a + e) // 2, (a + e) % 2
                a_ref[1 + mid + I + col, pl.ds(i, T), b * T:(b + 1) * T] = up(mid + I, e, a)
                m_ref[1 + mid + I + col, 2 * I + a, 0:1, b * T:(b + 1) * T] = mask_row(mid + I, e, a)
            for e in range(1, W):
                back, b = (a - e) // 2, (a - e) % 2
                a_ref[1 + mid + I + back, pl.ds(i, T), b * T:(b + 1) * T] = up(mid + I + back, e, b).T
                m_ref[1 + mid + I + back, 2 * I + a, 0:1, b * T:(b + 1) * T] = mask_row(mid + I + back, e, b)

    def super_tile(L, D):
        e = 2 * D
        if D == W // 2:
            top = jnp.concatenate([zero, zero], axis=1)
            low = jnp.concatenate([up(L, W - 1, 1), zero], axis=1)
        else:
            top = jnp.concatenate([up(L, e, 0), up(L, e + 1, 0)], axis=1)
            low = jnp.concatenate([up(L, e - 1, 1), up(L, e, 1)], axis=1)
        return jnp.concatenate([top, low], axis=0)

    def column(src, K):
        mirror = up(K, 1, 0)
        diag = jnp.concatenate(
            [jnp.concatenate([up(K, 0, 0), mirror], axis=1),
             jnp.concatenate([mirror.T, up(K, 0, 1)], axis=1)], axis=0)
        acc_ref[...] = jnp.dot(src[K + 1], diag, preferred_element_type=jnp.float32)
        for q in range(W // 4):
            near, far = 2 * q + 1, 2 * q + 2

            @pl.when(K - near >= 0)
            def _():
                left = jnp.concatenate([src[K + 1 - far], src[K + 1 - near]], axis=1)
                right = jnp.concatenate(
                    [super_tile(jnp.maximum(K - far, 0), far), super_tile(K - near, near)], axis=0)
                acc_ref[...] += jnp.dot(left, right, preferred_element_type=jnp.float32)

            @pl.when(K + far < NL)
            def _():
                left = jnp.concatenate([src[K + 1 + near], src[K + 1 + far]], axis=1)
                right = jnp.concatenate([super_tile(K, near), super_tile(K, far)], axis=1)
                acc_ref[...] += lax.dot_general(
                    left, right, (((1,), (1,)), ((), ())), preferred_element_type=jnp.float32)

            @pl.when(K + far == NL)
            def _():
                acc_ref[...] += lax.dot_general(
                    src[K + 1 + near], super_tile(K, near), (((1,), (1,)), ((), ())),
                    preferred_element_type=jnp.float32)

    @pl.loop(0, NL)
    def _(K):
        column(a_ref, K)
        for i in range(n):
            keep = m_ref[K + 1, i, 0:1, :] * scale
            p_ref[K + 1, i * T:(i + 1) * T, :] = (
                keep * acc_ref[i * T:(i + 1) * T, :]).astype(jnp.bfloat16)

    start = mid + r * (lw // 2)
    for jj in range((lw + n) // 2):
        column(p_ref, start + jj)
        for b in range(2):
            for i in range(n):
                t = 2 * jj + b - i
                if 0 <= t < lw:
                    cube = acc_ref[i * T:(i + 1) * T, b * T:(b + 1) * T]
                    own = g_ref[3 * half + i // 2, r, i % 2, t * T:(t + 1) * T, :].astype(jnp.float32)
                    keep = pat_ref[i, t].astype(jnp.float32) * 0.5
                    out_ref[i, t] = (keep * (3.0 * own - cube)).astype(jnp.bfloat16)


def on_device(R, C, matrix_band, pattern, filter_mask):
    n, lw, T, half = plan(matrix_band)
    W = lw * R
    rs = lw * T + 16
    bf = jnp.bfloat16
    window = pl.pallas_call(
        functools.partial(gather_kernel, R, C, n, lw, T),
        out_shape=jax.ShapeDtypeStruct((SLOTS * half, R, 2, rs, T), bf),
        in_specs=[
            pl.BlockSpec(memory_space=pltpu.VMEM),
            pl.BlockSpec(memory_space=pltpu.SMEM),
            pl.BlockSpec(memory_space=pltpu.SMEM),
        ],
        out_specs=pl.BlockSpec(memory_space=pl.ANY),
        scratch_shapes=[
            pltpu.VMEM((half, 2, rs, T), bf),
            pltpu.SemaphoreType.DMA((half,)),
            pltpu.SemaphoreType.DMA((SLOTS * half, R)),
            pltpu.SemaphoreType.DMA((3, half)),
            pltpu.SemaphoreType.DMA((4, half, R - 1)),
            pltpu.SemaphoreType.DMA((3, half, R)),
        ],
        compiler_params=pltpu.CompilerParams(
            collective_id=0, has_side_effects=True, vmem_limit_bytes=16 * 2**20),
    )(matrix_band, pattern, filter_mask)
    NL = SLOTS * half - 2
    return pl.pallas_call(
        functools.partial(compute_kernel, R, n, lw, T, W),
        out_shape=jax.ShapeDtypeStruct(matrix_band.shape, bf),
        in_specs=[
            pl.BlockSpec(memory_space=pltpu.VMEM),
            pl.BlockSpec(memory_space=pltpu.SMEM),
        ],
        out_specs=pl.BlockSpec(memory_space=pltpu.VMEM),
        scratch_shapes=[
            pltpu.VMEM((NL + 2, n * T, 2 * T), bf),
            pltpu.VMEM((NL + 2, n * T, 2 * T), bf),
            pltpu.VMEM((NL + 2, n, 8, 2 * T), jnp.float32),
            pltpu.VMEM((n * T, 2 * T), jnp.float32),
        ],
        compiler_params=pltpu.CompilerParams(vmem_limit_bytes=58 * 2**20),
    )(window, pattern)


def solution(mesh):
    placed = (P("col", "row", None, None), P("col", "row"), P("col", "row"))
    return jax.shard_map(
        functools.partial(on_device, mesh.shape["row"], mesh.shape["col"]),
        mesh=mesh,
        in_specs=placed,
        out_specs=P("col", "row", None, None),
        check_vma=False,
    )
```

time: 746 us -> 225 us (0.30)
  waiting for transfers between devices: 520 us -> 0 us
  Pallas kernels: 0 us -> 215 us
  local copies, waits for them, and re-layouts: 140 us -> 10.2 us
  matrix products: 36.4 us -> 0 us
  other arithmetic: 22.8 us -> 0 us
  between operations: 13.7 us -> 0.03 us
  starting transfers between devices: 10.8 us -> 0 us
    ppermute x9 -> x0, waiting for transfers between devices: 361 us -> none  [shifted(): return lax.ppermute(value, axis, pairs)]
    pallas_call x0 -> x2, Pallas kernels: none -> 215 us  [the longest x1 135 us: on_device(): pl.pallas_call(functools.partial(gather_kernel, R, C, n, lw, T), out_shap...]
    all_gather x2 -> x0, waiting for transfers between devices: 159 us -> none  [the longest x1 112 us: on_device(): square_own = lax.all_gather(square, 'row', axis=1, tiled=True)]
    unnamed x60 -> x8, local copies, waits for them, and re-layouts: 77.5 us -> 10.2 us
    another operation x18 -> x0, local copies, waits for them, and re-layouts: 43.5 us -> none  [whole_rows(): return jnp.concatenate([jnp.stack(mirrored, axis=1), upper_part], axis=1)]
    dot_general x8 -> x0, matrix products: 36.4 us -> none  [band_product(): jnp.einsum('iapq,iarq->ipr', left_block, right_block, preferred_element_t...]
    ppermute x9 -> x0, starting transfers between devices: 10.8 us -> none  [shifted(): return lax.ppermute(value, axis, pairs)]
    concatenate x1 -> x0, other arithmetic: 10.3 us -> none  [whole_rows(): return jnp.concatenate([jnp.stack(mirrored, axis=1), upper_part], axis=1)]
  transfers between devices with their start and end apart: 11 -> 0, of which waited for: 6 -> 0; matrix products, arithmetic and copies ran while one was open for 12% -> 0% of each run, Pallas kernels for 0% -> 0%
where the time goes in v1:
time: 225 us
  Pallas kernels  215 us (96%)
  local copies, waits for them, and re-layouts  10.2 us (5%)
    pallas_call x1, Pallas kernels, on_device(): pl.pallas_call(functools.partial(gather_kernel, R, C, n, lw, T), out_shap...  135 us
    pallas_call x1, Pallas kernels, on_device(): pl.pallas_call(functools.partial(compute_kernel, R, n, lw, T, W), out_sha...  79.7 us
    unnamed x8, local copies, waits for them, and re-layouts  10.2 us

profile of v1, /device:TPU:0, one launch (start us, length us, event | category | flops | bytes accessed | tf_op | source)
XLA Modules:
  0.0 224.9 jit_solution(3483591573185240734)
XLA Ops:
  0.0 0.8 copy.4.pat_ref
  0.8 0.0 copy-start.2
  0.8 0.8 copy.5.fm_ref
  1.5 0.0 copy-start.1
  1.5 1.1 copy-done.1
  2.7 135.1 %shard_map.37.g_ref = bf16[21,4,2,528,128]{4,3,2,1,0:T(8,128)(2,1)S(1)} custom-call(bf16[6,4,128,128]{3,2,1,0:T(8,128)(2,1)S(1)} %copy-done.1, s32[6,4]{1,0:T(8,128)S(1)} %copy.4.pat_ref, s32[6,4]{1,0:T(8,128)S(1)} %copy.5.fm_ref), custom_call_target="tpu_custom_call" | custom-call | tf_op jit(solution)/shard_map/pallas_call | solution.py:257
  137.8 0.0 copy-done.2
  137.8 0.0 copy-start
  137.8 7.5 %copy-done = bf16[21,4,2,528,128]{4,3,2,1,0:T(8,128)(2,1)} copy-done((bf16[21,4,2,528,128]{4,3,2,1,0:T(8,128)(2,1)}, bf16[21,4,2,528,128]{4,3,2,1,0:T(8,128)(2,1)S(1)}, u32[]{:S(2)}) %copy-start) | copy-done | bytes 22708248
  145.3 79.7 %shard_map.38 = bf16[6,4,128,128]{3,2,1,0:T(8,128)(2,1)} custom-call(bf16[21,4,2,528,128]{4,3,2,1,0:T(8,128)(2,1)} %copy-done, s32[6,4]{1,0:T(8,128)} %copy-done.2), custom_call_target="tpu_custom_call" | custom-call | tf_op jit(solution)/shard_map/pallas_call | solution.py:278
Async XLA Ops:
  0.8 137.0 %copy-start.2 = (s32[6,4]{1,0:T(8,128)}, s32[6,4]{1,0:T(8,128)S(1)}, u32[]{:S(2)}) copy-start(s32[6,4]{1,0:T(8,128)S(1)} %copy.4.pat_ref) | copy-start | bytes 292
  1.5 1.1 copy-start.1
  137.8 7.5 %copy-start = (bf16[21,4,2,528,128]{4,3,2,1,0:T(8,128)(2,1)}, bf16[21,4,2,528,128]{4,3,2,1,0:T(8,128)(2,1)S(1)}, u32[]{:S(2)}) copy-start(bf16[21,4,2,528,128]{4,3,2,1,0:T(8,128)(2,1)S(1)} %shard_map.37.g_ref) | copy-start | bytes 68124672

commit v2 on v1

--- a/solution.py
+++ b/solution.py
@@ -10,6 +10,8 @@
 
 MESH = pl.DeviceIdType.MESH
 SLOTS = 7
+GROUP = 4
+PAD = GROUP - 1
 
 
 def plan(matrix_band):
@@ -25,10 +27,14 @@
     sib = c + 1 - 2 * core
     right, left = lax.rem(c + 2, C), lax.rem(c + C - 2, C)
     third = lax.rem(c + C - 3 + 6 * core, C)
-    others = [lax.rem(r + d, R) for d in range(1, R)]
+    if R == 4:
+        side, over = r + 1 - 2 * lax.rem(r, 2), lax.rem(r + 2, 4)
+        near, others = [side, over], [side, over, lax.rem(side + 2, 4)]
+    else:
+        others = near = [lax.rem(r + d, R) for d in range(1, R)]
 
     barrier = pltpu.get_barrier_semaphore()
-    partners = [(r, sib), (r, right), (r, left), (r, third)] + [(o, c) for o in others]
+    partners = [(r, sib), (r, right), (r, left), (r, third)] + [(o, c) for o in near]
     for p in partners:
         pl.semaphore_signal(barrier, inc=1, device_id=p, device_id_type=MESH)
 
@@ -84,14 +90,14 @@
             start((core == 0) & g6(h, r),
                   lambda h=h: remote(own(h), 6 * half + h, r, zsend.at[2, h], (r, third)), sends)
     for h in range(half):
-        for d, o in enumerate(others):
+        for d, o in enumerate(near):
             start(True, lambda h=h, d=d, o=o: remote(own(h), 3 * half + h, r, rsend.at[3, h, d], (o, c)), sends)
         start(True, lambda h=h: remote(own(h), (4 * core + 2 * (1 - core)) * half + h, r,
                                        ssend.at[1, h, r], (r, sib)), sends)
         pltpu.make_async_copy(own(h), g_ref.at[3 * half + h, r], local_sem.at[h]).start()
 
     def to_row(cond, q, g, h):
-        for d, o in enumerate(others):
+        for d, o in enumerate(near):
             start(cond, lambda d=d, o=o: remote(g_ref.at[g, r], g, r, rsend.at[q, h, d], (o, c)), sends)
 
     def to_sib(q, s, h, rr):
@@ -106,6 +112,12 @@
             cond = low | ((core == 1) & (2 * h + rr * lw <= 3)) if h <= 1 else low
         start(cond, lambda: remote(g_ref.at[g, rr], dst, rr, ssend.at[q, h, rr], (r, sib)), sends)
 
+    def to_diagonal(cond, q, s, h, index):
+        if R != 4 or index != (s // 2 + h) % 2:
+            return
+        g, rr, dev = s * half + h, near[index], (near[1 - index], c)
+        start(cond, lambda: remote(g_ref.at[g, rr], g, rr, rsend.at[q, h, 2], dev), sends)
+
     for h in range(half):
         arrived(half + h, r)
         to_row(True, 0, half + h, h)
@@ -113,8 +125,9 @@
         when(g5(h, r), lambda h=h: arrived(5 * half + h, r))
         to_row(g5(h, r), 1, 5 * half + h, h)
         to_sib(2, 5, h, r)
-        for o in others:
+        for d, o in enumerate(others):
             arrived(3 * half + h, o)
+            to_diagonal(True, 3, 3, h, d)
             to_sib(1, 3, h, o)
     for h in range(half):
         if h >= 1:
@@ -125,17 +138,22 @@
             when(cond, lambda h=h: arrived(6 * half + h, r))
             to_row(cond, 2, 6 * half + h, h)
     for h in range(half):
-        for o in others:
+        for d, o in enumerate(others):
             arrived(half + h, o)
+            to_diagonal(True, 0, 1, h, d)
             to_sib(0, 1, h, o)
             when(g5(h, o), lambda h=h, o=o: arrived(5 * half + h, o))
+            to_diagonal(g5(h, o), 1, 5, h, d)
             to_sib(2, 5, h, o)
     for h in range(half):
-        for o in others:
+        for d, o in enumerate(others):
             if h >= 1:
                 when(core == 0, lambda h=h, o=o: arrived(h, o))
+                to_diagonal(core == 0, 2, 0, h, d)
             if h <= 1:
-                when((core == 1) & g6(h, o), lambda h=h, o=o: arrived(6 * half + h, o))
+                cond = (core == 1) & g6(h, o)
+                when(cond, lambda h=h, o=o: arrived(6 * half + h, o))
+                to_diagonal(cond, 2, 6, h, d)
     for h in range(half):
         for rr in range(R):
             arrived(2 * half + h, rr)
@@ -168,13 +186,14 @@
 
     zero = jnp.zeros((T, T), jnp.bfloat16)
 
-    @pl.loop(0, NL + 2)
+    @pl.loop(0, NL + 2 * PAD)
     def _(L):
         a_ref[L] = jnp.zeros((M, S), jnp.bfloat16)
         m_ref[L] = jnp.zeros((n, 8, S), jnp.float32)
 
-    p_ref[0] = jnp.zeros((M, S), jnp.bfloat16)
-    p_ref[NL + 1] = jnp.zeros((M, S), jnp.bfloat16)
+    for pad in range(PAD):
+        p_ref[pad] = jnp.zeros((M, S), jnp.bfloat16)
+        p_ref[NL + PAD + pad] = jnp.zeros((M, S), jnp.bfloat16)
 
     @pl.loop(0, half)
     def _(I):
@@ -182,12 +201,12 @@
             i = pl.multiple_of((2 * I + a) * T, T)
             for e in range(W):
                 col, b = (a + e) // 2, (a + e) % 2
-                a_ref[1 + mid + I + col, pl.ds(i, T), b * T:(b + 1) * T] = up(mid + I, e, a)
-                m_ref[1 + mid + I + col, 2 * I + a, 0:1, b * T:(b + 1) * T] = mask_row(mid + I, e, a)
+                a_ref[PAD + mid + I + col, pl.ds(i, T), b * T:(b + 1) * T] = up(mid + I, e, a)
+                m_ref[PAD + mid + I + col, 2 * I + a, 0:1, b * T:(b + 1) * T] = mask_row(mid + I, e, a)
             for e in range(1, W):
                 back, b = (a - e) // 2, (a - e) % 2
-                a_ref[1 + mid + I + back, pl.ds(i, T), b * T:(b + 1) * T] = up(mid + I + back, e, b).T
-                m_ref[1 + mid + I + back, 2 * I + a, 0:1, b * T:(b + 1) * T] = mask_row(mid + I + back, e, b)
+                a_ref[PAD + mid + I + back, pl.ds(i, T), b * T:(b + 1) * T] = up(mid + I + back, e, b).T
+                m_ref[PAD + mid + I + back, 2 * I + a, 0:1, b * T:(b + 1) * T] = mask_row(mid + I + back, e, b)
 
     def super_tile(L, D):
         e = 2 * D
@@ -199,46 +218,55 @@
             low = jnp.concatenate([up(L, e - 1, 1), up(L, e, 1)], axis=1)
         return jnp.concatenate([top, low], axis=0)
 
-    def column(src, K):
+    def column(src, K, lo, hi):
+        def left(*places):
+            parts = [src[place, lo:hi, :] for place in places]
+            return parts[0] if len(parts) == 1 else jnp.concatenate(parts, axis=1)
+
+        def mirrored(*distances):
+            parts = [super_tile(K, D) for D in distances]
+            right = parts[0] if len(parts) == 1 else jnp.concatenate(parts, axis=1)
+            acc_ref[lo:hi] += lax.dot_general(
+                left(*[K + PAD + D for D in distances]), right, (((1,), (1,)), ((), ())),
+                preferred_element_type=jnp.float32)
+
         mirror = up(K, 1, 0)
         diag = jnp.concatenate(
             [jnp.concatenate([up(K, 0, 0), mirror], axis=1),
              jnp.concatenate([mirror.T, up(K, 0, 1)], axis=1)], axis=0)
-        acc_ref[...] = jnp.dot(src[K + 1], diag, preferred_element_type=jnp.float32)
-        for q in range(W // 4):
-            near, far = 2 * q + 1, 2 * q + 2
-
-            @pl.when(K - near >= 0)
+        acc_ref[lo:hi] = jnp.dot(left(K + PAD), diag, preferred_element_type=jnp.float32)
+        for q in range(W // 2 // GROUP):
+            steps = [q * GROUP + D for D in range(1, GROUP + 1)]
+
+            @pl.when(K - steps[0] >= 0)
             def _():
-                left = jnp.concatenate([src[K + 1 - far], src[K + 1 - near]], axis=1)
                 right = jnp.concatenate(
-                    [super_tile(jnp.maximum(K - far, 0), far), super_tile(K - near, near)], axis=0)
-                acc_ref[...] += jnp.dot(left, right, preferred_element_type=jnp.float32)
-
-            @pl.when(K + far < NL)
+                    [super_tile(jnp.maximum(K - D, 0), D) for D in steps], axis=0)
+                acc_ref[lo:hi] += jnp.dot(
+                    left(*[K + PAD - D for D in steps]), right, preferred_element_type=jnp.float32)
+
+            @pl.when(K + steps[-1] < NL)
             def _():
-                left = jnp.concatenate([src[K + 1 + near], src[K + 1 + far]], axis=1)
-                right = jnp.concatenate([super_tile(K, near), super_tile(K, far)], axis=1)
-                acc_ref[...] += lax.dot_general(
-                    left, right, (((1,), (1,)), ((), ())), preferred_element_type=jnp.float32)
-
-            @pl.when(K + far == NL)
-            def _():
-                acc_ref[...] += lax.dot_general(
-                    src[K + 1 + near], super_tile(K, near), (((1,), (1,)), ((), ())),
-                    preferred_element_type=jnp.float32)
+                mirrored(*steps)
+
+            for D in steps[:-1]:
+                @pl.when((K + D < NL) & (K + steps[-1] >= NL))
+                def _(D=D):
+                    mirrored(D)
 
     @pl.loop(0, NL)
     def _(K):
-        column(a_ref, K)
+        column(a_ref, K, 0, M)
         for i in range(n):
-            keep = m_ref[K + 1, i, 0:1, :] * scale
-            p_ref[K + 1, i * T:(i + 1) * T, :] = (
+            keep = m_ref[K + PAD, i, 0:1, :] * scale
+            p_ref[K + PAD, i * T:(i + 1) * T, :] = (
                 keep * acc_ref[i * T:(i + 1) * T, :]).astype(jnp.bfloat16)
 
     start = mid + r * (lw // 2)
     for jj in range((lw + n) // 2):
-        column(p_ref, start + jj)
+        low = max(0, 2 * jj - lw + 1) // 2 * 2
+        high = min(n, 2 * jj + 2)
+        column(p_ref, start + jj, low * T, high * T)
         for b in range(2):
             for i in range(n):
                 t = 2 * jj + b - i
@@ -284,9 +312,9 @@
         ],
         out_specs=pl.BlockSpec(memory_space=pltpu.VMEM),
         scratch_shapes=[
-            pltpu.VMEM((NL + 2, n * T, 2 * T), bf),
-            pltpu.VMEM((NL + 2, n * T, 2 * T), bf),
-            pltpu.VMEM((NL + 2, n, 8, 2 * T), jnp.float32),
+            pltpu.VMEM((NL + 2 * PAD, n * T, 2 * T), bf),
+            pltpu.VMEM((NL + 2 * PAD, n * T, 2 * T), bf),
+            pltpu.VMEM((NL + 2 * PAD, n, 8, 2 * T), jnp.float32),
             pltpu.VMEM((n * T, 2 * T), jnp.float32),
         ],
         compiler_params=pltpu.CompilerParams(vmem_limit_bytes=58 * 2**20),

time: 225 us -> 206 us (0.916)
  Pallas kernels: 215 us -> 195 us
    pallas_call x1, Pallas kernels: 79.7 us -> 65.9 us  [on_device(): pl.pallas_call(functools.partial(compute_kernel, R, n, lw, T, W), out_sha...]
    pallas_call x1, Pallas kernels: 135 us -> 129 us  [on_device(): pl.pallas_call(functools.partial(gather_kernel, R, C, n, lw, T), out_shap...]
where the time goes in v2:
time: 206 us; the launch traced here: 205 us
  Pallas kernels  195 us (95%)
  local copies, waits for them, and re-layouts  10.2 us (5%)
    pallas_call x1, Pallas kernels, on_device(): pl.pallas_call(functools.partial(gather_kernel, R, C, n, lw, T), out_shap...  129 us
    pallas_call x1, Pallas kernels, on_device(): pl.pallas_call(functools.partial(compute_kernel, R, n, lw, T, W), out_sha...  65.9 us
    unnamed x8, local copies, waits for them, and re-layouts  10.2 us

profile of v2, /device:TPU:0, one launch (start us, length us, event | category | flops | bytes accessed | tf_op | source)
XLA Modules:
  0.0 205.5 jit_solution(2606642488533294496)
XLA Ops:
  0.0 0.8 copy.4.pat_ref
  0.8 0.0 copy-start.2
  0.8 0.8 copy.5.fm_ref
  1.5 0.0 copy-start.1
  1.5 1.1 copy-done.1
  2.7 129.4 %shard_map.37.g_ref = bf16[21,4,2,528,128]{4,3,2,1,0:T(8,128)(2,1)S(1)} custom-call(bf16[6,4,128,128]{3,2,1,0:T(8,128)(2,1)S(1)} %copy-done.1, s32[6,4]{1,0:T(8,128)S(1)} %copy.4.pat_ref, s32[6,4]{1,0:T(8,128)S(1)} %copy.5.fm_ref), custom_call_target="tpu_custom_call" | custom-call | tf_op jit(solution)/shard_map/pallas_call | solution.py:285
  132.1 0.0 copy-done.2
  132.1 0.0 copy-start
  132.1 7.5 %copy-done = bf16[21,4,2,528,128]{4,3,2,1,0:T(8,128)(2,1)} copy-done((bf16[21,4,2,528,128]{4,3,2,1,0:T(8,128)(2,1)}, bf16[21,4,2,528,128]{4,3,2,1,0:T(8,128)(2,1)S(1)}, u32[]{:S(2)}) %copy-start) | copy-done | bytes 22708248
  139.6 65.9 %shard_map.38 = bf16[6,4,128,128]{3,2,1,0:T(8,128)(2,1)} custom-call(bf16[21,4,2,528,128]{4,3,2,1,0:T(8,128)(2,1)} %copy-done, s32[6,4]{1,0:T(8,128)} %copy-done.2), custom_call_target="tpu_custom_call" | custom-call | tf_op jit(solution)/shard_map/pallas_call | solution.py:306
Async XLA Ops:
  0.8 131.3 %copy-start.2 = (s32[6,4]{1,0:T(8,128)}, s32[6,4]{1,0:T(8,128)S(1)}, u32[]{:S(2)}) copy-start(s32[6,4]{1,0:T(8,128)S(1)} %copy.4.pat_ref) | copy-start | bytes 292
  1.5 1.1 copy-start.1
  132.1 7.5 %copy-start = (bf16[21,4,2,528,128]{4,3,2,1,0:T(8,128)(2,1)}, bf16[21,4,2,528,128]{4,3,2,1,0:T(8,128)(2,1)S(1)}, u32[]{:S(2)}) copy-start(bf16[21,4,2,528,128]{4,3,2,1,0:T(8,128)(2,1)S(1)} %shard_map.37.g_ref) | copy-start | bytes 68124672

commit v3 on v2

--- a/solution.py
+++ b/solution.py
@@ -19,7 +19,10 @@
     return rows, width, tile, rows // 2
 
 
-def gather_kernel(R, C, n, lw, T, band_ref, pat_ref, fm_ref, g_ref, x_ref, local_sem, recv, zsend, rsend, ssend, ):
+def kernel(R, C, n, lw, T, W, band_ref, pat_ref, fm_ref, out_ref, g_ref, x_ref, a_ref, p_ref, m_ref, acc_ref,
+           local_sem, recv, zsend, rsend, ssend):
+    clear, left_panel, square_columns, cube = compute_steps(
+        R, n, lw, T, W, g_ref, pat_ref, out_ref, a_ref, p_ref, m_ref, acc_ref)
     r = lax.axis_index("row")
     c = lax.axis_index("col")
     core = lax.rem(c, 2)
@@ -118,6 +121,8 @@
         g, rr, dev = s * half + h, near[index], (near[1 - index], c)
         start(cond, lambda: remote(g_ref.at[g, rr], g, rr, rsend.at[q, h, 2], dev), sends)
 
+    clear()
+
     for h in range(half):
         arrived(half + h, r)
         to_row(True, 0, half + h, h)
@@ -157,18 +162,24 @@
     for h in range(half):
         for rr in range(R):
             arrived(2 * half + h, rr)
+            if h >= 1:
+                when(core == 1, lambda h=h, rr=rr: arrived(h, rr))
+        pltpu.make_async_copy(own(h), g_ref.at[3 * half + h, r], local_sem.at[h]).wait()
+    left_panel()
+    first = 4 * half - 1
+    square_columns(0, first)
+    for h in range(half):
+        for rr in range(R):
             when((core == 0) | (2 * h + rr * lw <= 15), lambda h=h, rr=rr: arrived(4 * half + h, rr))
             if h <= 1 and 2 * h + rr * lw <= 3:
                 when(core == 0, lambda h=h, rr=rr: arrived(6 * half + h, rr))
-            if h >= 1:
-                when(core == 1, lambda h=h, rr=rr: arrived(h, rr))
+    square_columns(first, SLOTS * half - 2)
+    cube()
     for cond, make in sends:
         when(cond, lambda make=make: make().wait_send())
-    for h in range(half):
-        pltpu.make_async_copy(own(h), g_ref.at[3 * half + h, r], local_sem.at[h]).wait()
-
-
-def compute_kernel(R, n, lw, T, W, g_ref, pat_ref, out_ref, a_ref, p_ref, m_ref, acc_ref):
+
+
+def compute_steps(R, n, lw, T, W, g_ref, pat_ref, out_ref, a_ref, p_ref, m_ref, acc_ref):
     r = lax.axis_index("row")
     S = 2 * T
     half = n // 2
@@ -186,27 +197,29 @@
 
     zero = jnp.zeros((T, T), jnp.bfloat16)
 
-    @pl.loop(0, NL + 2 * PAD)
-    def _(L):
-        a_ref[L] = jnp.zeros((M, S), jnp.bfloat16)
-        m_ref[L] = jnp.zeros((n, 8, S), jnp.float32)
-
-    for pad in range(PAD):
-        p_ref[pad] = jnp.zeros((M, S), jnp.bfloat16)
-        p_ref[NL + PAD + pad] = jnp.zeros((M, S), jnp.bfloat16)
-
-    @pl.loop(0, half)
-    def _(I):
-        for a in range(2):
-            i = pl.multiple_of((2 * I + a) * T, T)
-            for e in range(W):
-                col, b = (a + e) // 2, (a + e) % 2
-                a_ref[PAD + mid + I + col, pl.ds(i, T), b * T:(b + 1) * T] = up(mid + I, e, a)
-                m_ref[PAD + mid + I + col, 2 * I + a, 0:1, b * T:(b + 1) * T] = mask_row(mid + I, e, a)
-            for e in range(1, W):
-                back, b = (a - e) // 2, (a - e) % 2
-                a_ref[PAD + mid + I + back, pl.ds(i, T), b * T:(b + 1) * T] = up(mid + I + back, e, b).T
-                m_ref[PAD + mid + I + back, 2 * I + a, 0:1, b * T:(b + 1) * T] = mask_row(mid + I + back, e, b)
+    def clear():
+        @pl.loop(0, NL + 2 * PAD)
+        def _(L):
+            a_ref[L] = jnp.zeros((M, S), jnp.bfloat16)
+            m_ref[L] = jnp.zeros((n, 8, S), jnp.float32)
+
+        for pad in range(PAD):
+            p_ref[pad] = jnp.zeros((M, S), jnp.bfloat16)
+            p_ref[NL + PAD + pad] = jnp.zeros((M, S), jnp.bfloat16)
+
+    def left_panel():
+        @pl.loop(0, half)
+        def _(I):
+            for a in range(2):
+                i = pl.multiple_of((2 * I + a) * T, T)
+                for e in range(W):
+                    col, b = (a + e) // 2, (a + e) % 2
+                    a_ref[PAD + mid + I + col, pl.ds(i, T), b * T:(b + 1) * T] = up(mid + I, e, a)
+                    m_ref[PAD + mid + I + col, 2 * I + a, 0:1, b * T:(b + 1) * T] = mask_row(mid + I, e, a)
+                for e in range(1, W):
+                    back, b = (a - e) // 2, (a - e) % 2
+                    a_ref[PAD + mid + I + back, pl.ds(i, T), b * T:(b + 1) * T] = up(mid + I + back, e, b).T
+                    m_ref[PAD + mid + I + back, 2 * I + a, 0:1, b * T:(b + 1) * T] = mask_row(mid + I + back, e, b)
 
     def super_tile(L, D):
         e = 2 * D
@@ -254,27 +267,31 @@
                 def _(D=D):
                     mirrored(D)
 
-    @pl.loop(0, NL)
-    def _(K):
-        column(a_ref, K, 0, M)
-        for i in range(n):
-            keep = m_ref[K + PAD, i, 0:1, :] * scale
-            p_ref[K + PAD, i * T:(i + 1) * T, :] = (
-                keep * acc_ref[i * T:(i + 1) * T, :]).astype(jnp.bfloat16)
-
-    start = mid + r * (lw // 2)
-    for jj in range((lw + n) // 2):
-        low = max(0, 2 * jj - lw + 1) // 2 * 2
-        high = min(n, 2 * jj + 2)
-        column(p_ref, start + jj, low * T, high * T)
-        for b in range(2):
+    def square_columns(begin, end):
+        @pl.loop(begin, end)
+        def _(K):
+            column(a_ref, K, 0, M)
             for i in range(n):
-                t = 2 * jj + b - i
-                if 0 <= t < lw:
-                    cube = acc_ref[i * T:(i + 1) * T, b * T:(b + 1) * T]
-                    own = g_ref[3 * half + i // 2, r, i % 2, t * T:(t + 1) * T, :].astype(jnp.float32)
-                    keep = pat_ref[i, t].astype(jnp.float32) * 0.5
-                    out_ref[i, t] = (keep * (3.0 * own - cube)).astype(jnp.bfloat16)
+                keep = m_ref[K + PAD, i, 0:1, :] * scale
+                p_ref[K + PAD, i * T:(i + 1) * T, :] = (
+                    keep * acc_ref[i * T:(i + 1) * T, :]).astype(jnp.bfloat16)
+
+    def cube():
+        start = mid + r * (lw // 2)
+        for jj in range((lw + n) // 2):
+            low = max(0, 2 * jj - lw + 1) // 2 * 2
+            high = min(n, 2 * jj + 2)
+            column(p_ref, start + jj, low * T, high * T)
+            for b in range(2):
+                for i in range(n):
+                    t = 2 * jj + b - i
+                    if 0 <= t < lw:
+                        total = acc_ref[i * T:(i + 1) * T, b * T:(b + 1) * T]
+                        own = g_ref[3 * half + i // 2, r, i % 2, t * T:(t + 1) * T, :].astype(jnp.float32)
+                        keep = pat_ref[i, t].astype(jnp.float32) * 0.5
+                        out_ref[i, t] = (keep * (3.0 * own - total)).astype(jnp.bfloat16)
+
+    return clear, left_panel, square_columns, cube
 
 
 def on_device(R, C, matrix_band, pattern, filter_mask):
@@ -282,17 +299,23 @@
     W = lw * R
     rs = lw * T + 16
     bf = jnp.bfloat16
-    window = pl.pallas_call(
-        functools.partial(gather_kernel, R, C, n, lw, T),
-        out_shape=jax.ShapeDtypeStruct((SLOTS * half, R, 2, rs, T), bf),
+    NL = SLOTS * half - 2
+    return pl.pallas_call(
+        functools.partial(kernel, R, C, n, lw, T, W),
+        out_shape=jax.ShapeDtypeStruct(matrix_band.shape, bf),
         in_specs=[
             pl.BlockSpec(memory_space=pltpu.VMEM),
             pl.BlockSpec(memory_space=pltpu.SMEM),
             pl.BlockSpec(memory_space=pltpu.SMEM),
         ],
-        out_specs=pl.BlockSpec(memory_space=pl.ANY),
+        out_specs=pl.BlockSpec(memory_space=pltpu.VMEM),
         scratch_shapes=[
+            pltpu.VMEM((SLOTS * half, R, 2, rs, T), bf),
             pltpu.VMEM((half, 2, rs, T), bf),
+            pltpu.VMEM((NL + 2 * PAD, n * T, 2 * T), bf),
+            pltpu.VMEM((NL + 2 * PAD, n * T, 2 * T), bf),
+            pltpu.VMEM((NL + 2 * PAD, n, 8, 2 * T), jnp.float32),
+            pltpu.VMEM((n * T, 2 * T), jnp.float32),
             pltpu.SemaphoreType.DMA((half,)),
             pltpu.SemaphoreType.DMA((SLOTS * half, R)),
             pltpu.SemaphoreType.DMA((3, half)),
@@ -300,25 +323,8 @@
             pltpu.SemaphoreType.DMA((3, half, R)),
         ],
         compiler_params=pltpu.CompilerParams(
-            collective_id=0, has_side_effects=True, vmem_limit_bytes=16 * 2**20),
+            collective_id=0, has_side_effects=True, vmem_limit_bytes=58 * 2**20),
     )(matrix_band, pattern, filter_mask)
-    NL = SLOTS * half - 2
-    return pl.pallas_call(
-        functools.partial(compute_kernel, R, n, lw, T, W),
-        out_shape=jax.ShapeDtypeStruct(matrix_band.shape, bf),
-        in_specs=[
-            pl.BlockSpec(memory_space=pltpu.VMEM),
-            pl.BlockSpec(memory_space=pltpu.SMEM),
-        ],
-        out_specs=pl.BlockSpec(memory_space=pltpu.VMEM),
-        scratch_shapes=[
-            pltpu.VMEM((NL + 2 * PAD, n * T, 2 * T), bf),
-            pltpu.VMEM((NL + 2 * PAD, n * T, 2 * T), bf),
-            pltpu.VMEM((NL + 2 * PAD, n, 8, 2 * T), jnp.float32),
-            pltpu.VMEM((n * T, 2 * T), jnp.float32),
-        ],
-        compiler_params=pltpu.CompilerParams(vmem_limit_bytes=58 * 2**20),
-    )(window, pattern)
 
 
 def solution(mesh):

time: 206 us -> 192 us (0.932); the launches traced: 205 us -> 188 us
  Pallas kernels: 195 us -> 184 us
  local copies, waits for them, and re-layouts: 10.2 us -> 4.13 us
    pallas_call x2 -> x1, Pallas kernels: 195 us -> 184 us  [on_device(): pl.pallas_call(functools.partial(kernel, R, C, n, lw, T, W), out_shape=ja...]
    unnamed x8 -> x5, local copies, waits for them, and re-layouts: 10.2 us -> 4.13 us
where the time goes in v3:
time: 192 us; the launch traced here: 188 us
  Pallas kernels  184 us (96%)
  local copies, waits for them, and re-layouts  4.13 us (2%)
    pallas_call x1, Pallas kernels, on_device(): pl.pallas_call(functools.partial(kernel, R, C, n, lw, T, W), out_shape=ja...  184 us
    unnamed x5, local copies, waits for them, and re-layouts  4.13 us

profile of v3, /device:TPU:0, one launch (start us, length us, event | category | flops | bytes accessed | tf_op | source)
XLA Modules:
  0.0 188.3 jit_solution(18001375744498988231)
XLA Ops:
  0.0 0.0 copy-start
  0.0 1.4 copy.4.pat_ref
  1.4 0.0 copy-done
  1.4 0.7 copy.5.fm_ref
  2.0 184.1 %shard_map.37 = bf16[6,4,128,128]{3,2,1,0:T(8,128)(2,1)} custom-call(bf16[6,4,128,128]{3,2,1,0:T(8,128)(2,1)} %band_ref.1, s32[6,4]{1,0:T(8,128)} %copy.4.pat_ref, s32[6,4]{1,0:T(8,128)} %copy.5.fm_ref), custom_call_target="tpu_custom_call" | custom-call | tf_op jit(solution)/shard_map/pallas_call | solution.py:303
  186.2 2.1 %copy.7 = bf16[6,4,128,128]{3,2,1,0:T(8,128)(2,1)} copy(bf16[6,4,128,128]{3,2,1,0:T(8,128)(2,1)} %shard_map.37) | data formatting | bytes 1572864
Async XLA Ops:
  0.0 1.4 copy-start

commit v4 on v3

--- a/solution.py
+++ b/solution.py
@@ -127,9 +127,6 @@
         arrived(half + h, r)
         to_row(True, 0, half + h, h)
         to_sib(0, 1, h, r)
-        when(g5(h, r), lambda h=h: arrived(5 * half + h, r))
-        to_row(g5(h, r), 1, 5 * half + h, h)
-        to_sib(2, 5, h, r)
         for d, o in enumerate(others):
             arrived(3 * half + h, o)
             to_diagonal(True, 3, 3, h, d)
@@ -143,13 +140,14 @@
             when(cond, lambda h=h: arrived(6 * half + h, r))
             to_row(cond, 2, 6 * half + h, h)
     for h in range(half):
+        when(g5(h, r), lambda h=h: arrived(5 * half + h, r))
+        to_row(g5(h, r), 1, 5 * half + h, h)
+        to_sib(2, 5, h, r)
+    for h in range(half):
         for d, o in enumerate(others):
             arrived(half + h, o)
             to_diagonal(True, 0, 1, h, d)
             to_sib(0, 1, h, o)
-            when(g5(h, o), lambda h=h, o=o: arrived(5 * half + h, o))
-            to_diagonal(g5(h, o), 1, 5, h, d)
-            to_sib(2, 5, h, o)
     for h in range(half):
         for d, o in enumerate(others):
             if h >= 1:
@@ -167,7 +165,12 @@
         pltpu.make_async_copy(own(h), g_ref.at[3 * half + h, r], local_sem.at[h]).wait()
     left_panel()
     first = 4 * half - 1
-    square_columns(0, first)
+    for h in range(half):
+        for d, o in enumerate(others):
+            when(g5(h, o), lambda h=h, o=o: arrived(5 * half + h, o))
+            to_diagonal(g5(h, o), 1, 5, h, d)
+            to_sib(2, 5, h, o)
+        square_columns(h * first // half, (h + 1) * first // half)
     for h in range(half):
         for rr in range(R):
             when((core == 0) | (2 * h + rr * lw <= 15), lambda h=h, rr=rr: arrived(4 * half + h, rr))

time: 192 us -> 199 us (1.036)
  the two profiles are of different devices: /device:TPU:0 before, /device:TPU:14 now
where the time goes in v4:
time: 199 us
  Pallas kernels  194 us (97%)
  local copies, waits for them, and re-layouts  4.13 us (2%)
    pallas_call x1, Pallas kernels, on_device(): pl.pallas_call(functools.partial(kernel, R, C, n, lw, T, W), out_shape=ja...  194 us
    unnamed x5, local copies, waits for them, and re-layouts  4.13 us

profile of v4, /device:TPU:14, one launch (start us, length us, event | category | flops | bytes accessed | tf_op | source)
XLA Modules:
  0.0 198.6 jit_solution(5175289078857253005)
XLA Ops:
  0.0 0.0 copy-start
  0.0 1.4 copy.4.pat_ref
  1.4 0.0 copy-done
  1.4 0.7 copy.5.fm_ref
  2.0 194.5 %shard_map.37 = bf16[6,4,128,128]{3,2,1,0:T(8,128)(2,1)} custom-call(bf16[6,4,128,128]{3,2,1,0:T(8,128)(2,1)} %band_ref.1, s32[6,4]{1,0:T(8,128)} %copy.4.pat_ref, s32[6,4]{1,0:T(8,128)} %copy.5.fm_ref), custom_call_target="tpu_custom_call" | custom-call | tf_op jit(solution)/shard_map/pallas_call | solution.py:306
  196.5 2.1 %copy.7 = bf16[6,4,128,128]{3,2,1,0:T(8,128)(2,1)} copy(bf16[6,4,128,128]{3,2,1,0:T(8,128)(2,1)} %shard_map.37) | data formatting | bytes 1572864
Async XLA Ops:
  0.0 1.4 copy-start
